TPU v7x, 32 devices: a whole 2x2x4 slice. The times are simulated.
32 devices in a mesh: group: 2 (over y), space: 4 (over z), dp: 2 (over core), mp: 2 (over x).
Axes of the slice: x: 2, y: 2, z: 4, core: 2. Of those that a mesh axis runs over, the one named last changes fastest.
Arguments:
- node_latent: bfloat16 [4, 1024, 512], P(('group', 'dp'), 'space'), parts along dimension 0, may hold values from -6 to 6
- halo_latent: bfloat16 [4, 1024, 512], P(('group', 'dp'), 'space'), parts along dimension 0, may hold values from -6 to 6
- coarse_latent: bfloat16 [4, 32, 512], P(('group', 'dp')), parts along dimension 0, may hold values from -6 to 6
- edge_latent: bfloat16 [4, 2048, 512], P(('group', 'dp'), 'space'), parts along dimension 0, may hold values from -6 to 6
- edge_preact: bfloat16 [4, 2048, 512], P(('group', 'dp'), 'space', 'mp'), parts along dimension 0, may hold values from -6 to 6
- edge_mixed: bfloat16 [4, 2048, 512], P(('group', 'dp'), 'space'), parts along dimension 0, may hold values from -6 to 6
- node_message: bfloat16 [4, 1024, 512], P(('group', 'dp'), 'space'), parts along dimension 0, may hold values from -12 to 12
- node_preact: bfloat16 [4, 1024, 512], P(('group', 'dp'), 'space', 'mp'), parts along dimension 0, may hold values from -6 to 6
- node_mixed: bfloat16 [4, 1024, 512], P(('group', 'dp'), 'space'), parts along dimension 0, may hold values from -6 to 6
- edge_cotangent: bfloat16 [4, 2048, 512], P(('group', 'dp'), 'space'), parts along dimension 0, may hold values from -6 to 6
- node_cotangent: bfloat16 [4, 1024, 512], P(('group', 'dp'), 'space'), parts along dimension 0, may hold values from -6 to 6
- senders: int32 [2048], P('space'), may hold values from 0 to 543
- receivers: int32 [2048], P('space'), may hold values from 0 to 255
- send_rows: int32 [4, 2, 128], P('space'), may hold values from 0 to 255
- coarse_rows: int32 [32], replicated, may hold values from 0 to 255
- edge_up: bfloat16 [1536, 512], P(None, 'mp'), may hold values from -0.15625 to 0.15625
- edge_down: bfloat16 [512, 512], P('mp'), may hold values from -0.25 to 0.25
- edge_gain: float32 [512], replicated, may hold values from 0.1 to 1.9
- node_up: bfloat16 [1024, 512], P(None, 'mp'), may hold values from -0.1875 to 0.1875
- node_down: bfloat16 [512, 512], P('mp'), may hold values from -0.25 to 0.25
- node_gain: float32 [512], replicated, may hold values from 0.1 to 1.9
Outputs:
- node_grad: bfloat16 [4, 1024, 512], P(('group', 'dp'), 'space', 'mp'), parts along dimension 0
- edge_grad: bfloat16 [4, 2048, 512], P(('group', 'dp'), 'space', 'mp'), parts along dimension 0
- edge_upgrad: bfloat16 [3072, 512], P('group', 'mp'), parts along dimension 0
- edge_downgrad: bfloat16 [1024, 512], P(('group', 'mp')), parts along dimension 0
- node_upgrad: bfloat16 [2048, 512], P('group', 'mp'), parts along dimension 0
- node_downgrad: bfloat16 [1024, 512], P(('group', 'mp')), parts along dimension 0
- edge_gaingrad: float32 [1024], P('group'), parts along dimension 0
- node_gaingrad: float32 [1024], P('group'), parts along dimension 0
There are 2 independent parts, one for each index of `group`. A program takes and returns all parts, laid end to end along the dimension named above; an argument that names none is the same for every part. Nothing has to cross between parts.
Inputs may be any that keep to these rules, and one draw needn't show every extreme that they name: `senders`: a row of the edge's region's extended table. `receivers`: a row among the edge's region's own nodes. `send_rows`: rows among the sending region's own nodes. `coarse_rows`: coarse node c is owned by region c // 8; the entry is a row among that region's own nodes, below 256.
All inputs are finite; a program needn't handle non-finite values.
Results may differ from a plain program's by a relative error of at most 0.015.
Values may be sent and summed in bfloat16 or wider, within the bound.
A program may use at most 64 MiB of HBM per device.

v0:
```python
import math

import jax
import jax.numpy as jnp
from jax import lax
from jax.sharding import PartitionSpec as P

EPSILON = 1e-05


def passed_along(value, axis, steps):
    count = lax.axis_size(axis)
    pairs = [(source, (source + steps) % count) for source in range(count)]
    return lax.ppermute(value, axis, pairs)


def silu_slope(preact):
    logistic = jax.nn.sigmoid(preact)
    return logistic * (1.0 + preact * (1.0 - logistic))


def norm_back(mixed, norm_gain, upstream):
    values = mixed.astype(jnp.float32)
    centred = values - jnp.mean(values, -1, keepdims=True)
    inverse = lax.rsqrt(jnp.mean(centred * centred, -1, keepdims=True) + EPSILON)
    normed = centred * inverse
    scaled = upstream * norm_gain
    mix_delta = inverse * (
        scaled
        - jnp.mean(scaled, -1, keepdims=True)
        - normed * jnp.mean(scaled * normed, -1, keepdims=True)
    )
    return (mix_delta, normed)


def last_dot(left, right):
    return lax.dot_general(
        left, right, (((1,), (1,)), ((), ())), preferred_element_type=jnp.float32
    )


def first_dot(left, right):
    return lax.dot_general(
        left, right, (((0,), (0,)), ((), ())), preferred_element_type=jnp.float32
    )


def onehot_sum(index, count, values):
    pattern = (
        lax.broadcasted_iota(jnp.int32, (count, index.shape[0]), 0) == index[None, :]
    ).astype(jnp.bfloat16)
    high_part = lax.optimization_barrier(values.astype(jnp.bfloat16))
    low_part = (values - high_part.astype(jnp.float32)).astype(jnp.bfloat16)
    return jnp.dot(pattern, high_part, preferred_element_type=jnp.float32) + jnp.dot(
        pattern, low_part, preferred_element_type=jnp.float32
    )


def body(
    node_latent,
    halo_latent,
    coarse_latent,
    edge_latent,
    edge_preact,
    edge_mixed,
    node_message,
    node_preact,
    node_mixed,
    edge_cotangent,
    node_cotangent,
    senders,
    receivers,
    send_rows,
    coarse_rows,
    edge_up,
    edge_down,
    edge_gain,
    node_up,
    node_down,
    node_gain,
):
    width = node_latent.shape[2]
    node_rows = node_latent.shape[1]
    edge_count = edge_latent.shape[1]
    halo_rows = halo_latent.shape[1] // 2
    quarter = width // lax.axis_size("mp")
    feature_start = lax.axis_index("mp") * quarter
    own_nodes = node_latent[0]
    node_upstream = node_cotangent[0].astype(jnp.float32)
    node_delta, node_normed = norm_back(node_mixed[0], node_gain, node_upstream)
    node_gainsum = jnp.sum(node_upstream * node_normed, 0)
    node_delta = node_delta.astype(jnp.bfloat16)
    node_act = node_preact[0].astype(jnp.float32)
    node_hidden = jax.nn.silu(node_act).astype(jnp.bfloat16)
    node_signal = (last_dot(node_delta, node_down) * silu_slope(node_act)).astype(jnp.bfloat16)
    node_downsum = first_dot(node_hidden, node_delta)
    node_upsum = jnp.concatenate(
        [first_dot(own_nodes, node_signal), first_dot(node_message[0], node_signal)], 0
    )
    node_total = lax.psum(last_dot(node_signal, node_up), "mp")
    message_grad = node_total[:, width:]
    edge_upstream = edge_cotangent[0].astype(jnp.float32) + jnp.take(
        message_grad, receivers, axis=0
    )
    edge_delta, edge_normed = norm_back(edge_mixed[0], edge_gain, edge_upstream)
    edge_gainsum = jnp.sum(edge_upstream * edge_normed, 0)
    edge_delta = edge_delta.astype(jnp.bfloat16)
    edge_act = edge_preact[0].astype(jnp.float32)
    edge_hidden = jax.nn.silu(edge_act).astype(jnp.bfloat16)
    edge_signal = (last_dot(edge_delta, edge_down) * silu_slope(edge_act)).astype(jnp.bfloat16)
    extended = jnp.concatenate([own_nodes, halo_latent[0], coarse_latent[0]], 0)
    sender_latent = jnp.take(extended, senders, axis=0)
    receiver_latent = jnp.take(own_nodes, receivers, axis=0)
    edge_upsum = jnp.concatenate(
        [
            first_dot(edge_latent[0], edge_signal),
            first_dot(sender_latent, edge_signal),
            first_dot(receiver_latent, edge_signal),
        ],
        0,
    )
    edge_downsum = first_dot(edge_hidden, edge_delta)
    edge_terms = last_dot(edge_signal, edge_up).reshape(edge_count, 3, width)
    pieces = lax.psum_scatter(
        edge_terms.astype(jnp.bfloat16), "mp", scatter_dimension=2, tiled=True
    ).astype(jnp.float32)
    edge_grad = (
        lax.dynamic_slice_in_dim(edge_cotangent[0], feature_start, quarter, 1).astype(jnp.float32)
        + pieces[:, 0]
    ).astype(jnp.bfloat16)
    ext_grad = onehot_sum(senders, extended.shape[0], pieces[:, 1])
    node_sum = lax.dynamic_slice_in_dim(node_cotangent[0], feature_start, quarter, 1).astype(
        jnp.float32
    )
    node_sum = node_sum + lax.dynamic_slice_in_dim(node_total, feature_start, quarter, 1)
    node_sum = node_sum + onehot_sum(receivers, node_rows, pieces[:, 2]) + ext_grad[:node_rows]
    for slot, offset in enumerate((-1, 1)):
        block = ext_grad[node_rows + slot * halo_rows : node_rows + (slot + 1) * halo_rows]
        moved = passed_along(block.astype(jnp.bfloat16), "space", offset).astype(block.dtype)
        node_sum = node_sum + onehot_sum(send_rows[0, slot], node_rows, moved)
    coarse_grad = ext_grad[node_rows + 2 * halo_rows :]
    region = lax.axis_index("space")
    per_region = coarse_grad.shape[0] // lax.axis_size("space")
    coarse_total = lax.psum(coarse_grad.astype(jnp.bfloat16), "space").astype(jnp.float32)
    owner = lax.broadcasted_iota(jnp.int32, (coarse_grad.shape[0],), 0) // per_region
    owned_rows = jnp.where(owner == region, coarse_rows, -1)
    node_sum = node_sum + onehot_sum(owned_rows, node_rows, coarse_total)
    totals = lax.psum(
        (edge_upsum, edge_downsum, node_upsum, node_downsum, edge_gainsum, node_gainsum),
        ("space", "dp"),
    )
    sample_count = node_latent.shape[0] * lax.axis_size("dp")
    edge_scale = 1.0 / math.sqrt(sample_count * edge_count * lax.axis_size("space"))
    node_scale = 1.0 / math.sqrt(sample_count * node_rows * lax.axis_size("space"))
    return (
        node_sum.astype(jnp.bfloat16)[None],
        edge_grad[None],
        (totals[0] * edge_scale).astype(jnp.bfloat16),
        (totals[1] * edge_scale).astype(jnp.bfloat16),
        (totals[2] * node_scale).astype(jnp.bfloat16),
        (totals[3] * node_scale).astype(jnp.bfloat16),
        totals[4] * edge_scale,
        totals[5] * node_scale,
    )


def solution(mesh):
    return jax.shard_map(
        body,
        mesh=mesh,
        in_specs=(
            P(("group", "dp"), "space", None),
            P(("group", "dp"), "space", None),
            P(("group", "dp"), None, None),
            P(("group", "dp"), "space", None),
            P(("group", "dp"), "space", "mp"),
            P(("group", "dp"), "space", None),
            P(("group", "dp"), "space", None),
            P(("group", "dp"), "space", "mp"),
            P(("group", "dp"), "space", None),
            P(("group", "dp"), "space", None),
            P(("group", "dp"), "space", None),
            P("space"),
            P("space"),
            P("space", None, None),
            P(),
            P(None, "mp"),
            P("mp", None),
            P(),
            P(None, "mp"),
            P("mp", None),
            P(),
        ),
        out_specs=(
            P(("group", "dp"), "space", "mp"),
            P(("group", "dp"), "space", "mp"),
            P("group", "mp"),
            P(("group", "mp"), None),
            P("group", "mp"),
            P(("group", "mp"), None),
            P("group"),
            P("group"),
        ),
        check_vma=False,
    )
```

profile of v0, /device:TPU:0, one launch (start us, length us, event | category | flops | bytes accessed | tf_op | source)
XLA Modules:
  0.0 227.7 jit_solution(9405490456293881785)
XLA Ops:
  7.2 1.1 convert_reduce_fusion.1
  8.4 1.2 fusion.57
  9.5 1.4 fusion.43
  11.0 1.6 fusion.7
  12.6 1.3 fusion.139
  15.1 2.6 %gather_fusion.2 = bf16[512,512]{1,0:T(8,128)(2,1)} fusion(bf16[256,512]{1,0:T(8,128)(2,1)S(1)} %bitcast.206, s32[1024]{0:T(1024)S(1)} %pad_clamp_fusion.1), kind=kCustom, calls=%fused_computation.2 | custom fusion | bytes 1050624 | tf_op jit(solution)/shard_map/jit(_take)/gather | solution.py:113
  17.8 2.6 %gather_fusion.1 = bf16[512,512]{1,0:T(8,128)(2,1)} fusion(bf16[544,512]{1,0:T(8,128)(2,1)S(1)} %pad_maximum_fusion.2, s32[1024]{0:T(1024)S(1)} %pad_clamp_fusion), kind=kCustom, calls=%fused_computation.1 | custom fusion | bytes 1050624 | tf_op jit(solution)/shard_map/jit(_take)/gather | solution.py:112
  20.4 1.1 pad_maximum_fusion.1
  21.7 1.3 fusion.99
  23.0 33.8 %all-reduce.5.cloned.1.call-done = f32[256,1024]{1,0:T(8,128)} async-done(((f32[256,1024]{1,0:T(8,128)}), f32[256,1024]{1,0:T(8,128)}) %all-reduce.5.cloned.1.call-update) | async-done | bytes 1048592 | tf_op jit(solution)/shard_map/psum | solution.py:100
  56.8 1.0 slice-done
  57.9 1.6 gather_fusion
  59.5 1.8 fusion.26
  61.3 1.7 fusion.67
  63.0 0.7 fusion
  64.1 0.4 fusion.70
  64.5 0.6 copy-done.14
  65.4 0.4 fusion.72
  65.8 1.3 pad_maximum_fusion
  67.2 0.6 convolution_convert_fusion
  67.8 1.6 copy.34
  69.4 1.0 copy-done.7
  70.4 0.8 copy.43
  71.3 0.6 compare_select_fusion.2
  71.9 0.5 slice_bitcast_fusion.3
  72.4 17.2 %all-reduce = (f32[512]{0:T(512)S(1)}, f32[512]{0:T(512)S(1)}) all-reduce(f32[512]{0:T(512)S(1)} %get-tuple-element.24, f32[512]{0:T(512)S(1)} %get-tuple-element.27), channel_id=1, replica_groups=mesh['group'=2,'space'=4,'dp'=2,'mp'=2] {'space','dp'}, use_global_device_ids=true, to_apply=%region_16.17 | all-reduce | flops 1024 | bytes 8192 | tf_op jit(solution)/shard_map/psum | solution.py:148
  89.6 0.6 broadcast_multiply_fusion.1
  90.2 0.6 broadcast_multiply_fusion
  90.8 64.6 %all-reduce.7.cloned.1.call-done = (f32[1536,256]{0,1:T(8,128)}, f32[256,512]{1,0:T(8,128)}, f32[1024,256]{0,1:T(8,128)}, f32[256,512]{1,0:T(8,128)}) async-done(((f32[1536,256]{0,1:T(8,128)}, f32[256,512]{1,0:T(8,128)}, f32[1024,256]{0,1:T(8,128)}, f32[256,512]{1,0:T(8,128)}), (f32[1536,256]{0,1:T(8,128)}, f32[256,512]{1,0:T(8,128)}, f32[1024,256]{0,1:T(8,128)}, ...) | async-done | bytes 3670032 | tf_op jit(solution)/shard_map/psum | solution.py:148
  155.3 1.6 multiply_convert_fusion
  156.9 1.2 copy.39
  158.2 1.0 copy.40
  159.2 1.8 multiply_convert_fusion.3
  161.0 0.7 multiply_convert_fusion.2
  161.7 22.1 %reduce-scatter.2.cloned.1.call-done = bf16[512,3,256]{0,2,1:T(8,128)(2,1)} async-done(((bf16[512,3,512]{0,2,1:T(8,128)(2,1)}), bf16[512,3,256]{0,2,1:T(8,128)(2,1)}) %reduce-scatter.2.cloned.1.call-update) | async-done | bytes 786448 | tf_op jit(solution)/shard_map/reduce_scatter | solution.py:124
  183.8 1.3 convert_element_type.198
  185.6 1.2 fusion.138
  186.8 0.7 fusion.137
  187.4 0.6 slice.55
  188.0 1.0 fusion.79
  189.0 3.3 %collective-permute-start = (bf16[128,256]{1,0:T(8,128)(2,1)}, bf16[128,256]{1,0:T(8,128)(2,1)S(1)}, u32[]{:S(2)}, u32[]{:S(2)}) collective-permute-start(bf16[128,256]{1,0:T(8,128)(2,1)} %get-tuple-element.39), channel_id=1, source_target_pairs={{0,12},{4,0},{8,4},{12,8},{1,13},{5,1},{9,5},{13,9},{2,14},{6,2},{... | collective-permute-start | bytes 196616 | tf_op jit(solution)/shard_map/ppermute | solution.py:14
  192.3 19.8 %psum.57 = bf16[32,256]{1,0:T(8,128)(2,1)S(1)} all-reduce(bf16[32,256]{1,0:T(8,128)(2,1)} %slice.55), channel_id=1, replica_groups=mesh['group'=2,'space'=4,'dp'=2,'mp'=2] {'space'}, use_global_device_ids=true, to_apply=%region_10.11 | all-reduce | flops 8192 | bytes 32768 | tf_op jit(solution)/shard_map/psum | solution.py:144
  212.2 1.7 fusion.66
  213.9 2.1 fusion.2
  216.2 1.8 copy.38
  218.0 0.8 fusion.123
  218.8 1.1 fusion.5
  220.3 0.8 fusion.8
  (94 shorter events, 3.2 us)
Async XLA Ops:
  7.2 60.0 %copy-start = (bf16[1536,256]{1,0:T(8,128)(2,1)S(1)}, bf16[1536,256]{1,0:T(8,128)(2,1)}, u32[]{:S(2)}) copy-start(bf16[1536,256]{1,0:T(8,128)(2,1)} %param.36) | copy-start | bytes 2359300
  7.2 49.6 %all-reduce.5.cloned.1.call-start = ((), (), s32[]{:S(2)}) async-start(), calls=%async_computation.1 | async-start | bytes 2097152 | tf_op jit(solution)/shard_map/psum | solution.py:100
  10.9 1.6 copy-start.13
  12.5 1.4 copy-start.3
  12.5 1.9 copy-start.19
  12.6 1.9 copy-start.17
  12.6 1.9 copy-start.15
  13.9 0.9 copy-start.2
  13.9 141.4 %all-reduce.7.cloned.1.call-start = ((), (), s32[]{:S(2)}) async-start(), calls=%async_computation.3 | async-start | bytes 7340032 | tf_op jit(solution)/shard_map/psum | solution.py:148
  15.1 2.7 %copy-start.16 = (bf16[1,256,512]{2,1,0:T(8,128)(2,1)S(1)}, bf16[1,256,512]{2,1,0:T(8,128)(2,1)}, u32[]{:S(2)}) copy-start(bf16[1,256,512]{2,1,0:T(8,128)(2,1)} %param.22) | copy-start | bytes 786436
  15.1 2.6 %copy-start.18 = (bf16[1,32,512]{2,1,0:T(8,128)(2,1)S(1)}, bf16[1,32,512]{2,1,0:T(8,128)(2,1)}, u32[]{:S(2)}) copy-start(bf16[1,32,512]{2,1,0:T(8,128)(2,1)} %param.23) | copy-start | bytes 98308
  20.4 1.1 copy-start.4
  20.4 1.1 copy-start.9
  20.4 1.2 copy-start.21
  20.4 1.3 copy-start.28
  56.8 1.0 slice-start
  57.9 1.6 copy-start.22
  59.5 1.8 copy-start.6
  59.5 1.8 copy-start.27
  61.3 1.7 copy-start.26
  63.0 1.0 copy-start.11
  64.1 1.0 copy-start.14
  64.1 1.4 copy-start.10
  67.1 116.7 %reduce-scatter.2.cloned.1.call-start = ((), (), s32[]{:S(2)}) async-start(), calls=%async_computation.2 | async-start | bytes 2359296 | tf_op jit(solution)/shard_map/reduce_scatter | solution.py:124
  69.4 1.0 copy-start.7
  69.4 1.9 copy-start.29
  69.4 2.5 %copy-start.25 = (s32[1,2,128]{2,1,0:T(2,128)S(1)}, s32[1,2,128]{2,1,0:T(2,128)}, u32[]{:S(2)}) copy-start(s32[1,2,128]{2,1,0:T(2,128)} %param.34) | copy-start | bytes 3076
  155.3 2.8 %copy-start.8 = (f32[1024,256]{0,1:T(8,128)S(1)}, f32[1024,256]{0,1:T(8,128)}, u32[]{:S(2)}) copy-start(f32[1024,256]{0,1:T(8,128)} %get-tuple-element.34) | copy-start | bytes 3145732
  158.1 2.9 %copy-start.12 = (f32[256,512]{1,0:T(8,128)S(1)}, f32[256,512]{1,0:T(8,128)}, u32[]{:S(2)}) copy-start(f32[256,512]{1,0:T(8,128)} %get-tuple-element.35) | copy-start | bytes 1572868
  185.2 2.8 %copy-start.5 = (bf16[512,256]{0,1:T(8,128)(2,1)}, bf16[512,256]{0,1:T(8,128)(2,1)S(1)}, u32[]{:S(2)}) copy-start(bf16[512,256]{0,1:T(8,128)(2,1)S(1)} %get-tuple-element.37) | copy-start | bytes 786436
  185.6 28.3 %copy-start.1 = (f32[256,1024]{1,0:T(8,128)S(1)}, f32[256,1024]{1,0:T(8,128)}, u32[]{:S(2)}) copy-start(f32[256,1024]{1,0:T(8,128)} %all-reduce.5.cloned.1.call-done) | copy-start | bytes 3145732
  189.0 29.0 %collective-permute-start = (bf16[128,256]{1,0:T(8,128)(2,1)}, bf16[128,256]{1,0:T(8,128)(2,1)S(1)}, u32[]{:S(2)}, u32[]{:S(2)}) collective-permute-start(bf16[128,256]{1,0:T(8,128)(2,1)} %get-tuple-element.39), channel_id=1, source_target_pairs={{0,12},{4,0},{8,4},{12,8},{1,13},{5,1},{9,5},{13,9},{2,14},{6,2},{... | collective-permute-start | bytes 196616 | tf_op jit(solution)/shard_map/ppermute | solution.py:14
  192.3 27.6 %collective-permute-start.1 = (bf16[128,256]{1,0:T(8,128)(2,1)}, bf16[128,256]{1,0:T(8,128)(2,1)S(1)}, u32[]{:S(2)}, u32[]{:S(2)}) collective-permute-start(bf16[128,256]{1,0:T(8,128)(2,1)} %get-tuple-element.38), channel_id=1, source_target_pairs={{0,4},{4,8},{8,12},{12,0},{1,5},{5,9},{9,13},{13,1},{2,6},{6,10},{... | collective-permute-start | bytes 196616 | tf_op jit(solution)/shard_map/ppermute | solution.py:14
  212.2 3.9 %copy-start.23 = (s32[32]{0:T(128)S(1)}, s32[32]{0:T(128)}, u32[]{:S(2)}) copy-start(s32[32]{0:T(128)} %compare_select_fusion.2) | copy-start | bytes 388
  216.0 3.9 %copy-start.20 = (s32[128]{0:T(128)S(1)}, s32[128]{0:T(128)}, u32[]{:S(2)}) copy-start(s32[128]{0:T(128)} %get-tuple-element.40) | copy-start | bytes 1540
  216.0 4.3 %copy-start.24 = (s32[32]{0:T(128)S(1)}, s32[32]{0:T(128)}, u32[]{:S(2)}) copy-start(s32[32]{0:T(128)} %compare_select_fusion.2) | copy-start | bytes 388
Sparse Core Ops, SparseCore 0:
  14.0 42.7 all-reduce.4
  67.3 88.0 all-reduce.6
  157.7 26.0 reduce-scatter.1
where the time goes:
time: 228 us
  waiting for transfers between devices  120 us (53%)
  blocking collectives  37 us (16%)
  local copies, waits for them, and re-layouts  18.4 us (8%)
  other arithmetic  17.4 us (8%)
  matrix products  16.7 us (7%)
  between operations  14.2 us (6%)
  starting transfers between devices  3.45 us (2%)
    psum x1, waiting for transfers between devices, body(): lax.psum((edge_upsum, edge_downsum, node_upsum, node_downsum, edge_gainsu...  64.6 us
    psum x1, waiting for transfers between devices, body(): node_total = lax.psum(last_dot(node_signal, node_up), 'mp')  33.8 us
    reduce_scatter x1, waiting for transfers between devices, body(): lax.psum_scatter(edge_terms.astype(jnp.bfloat16), 'mp', scatter_dimension...  22.1 us
    psum x1, blocking collectives, body(): lax.psum(coarse_grad.astype(jnp.bfloat16), 'space').astype(jnp.float32)  19.8 us
    psum x1, blocking collectives, body(): lax.psum((edge_upsum, edge_downsum, node_upsum, node_downsum, edge_gainsu...  17.2 us
    unnamed x64, local copies, waits for them, and re-layouts  7.05 us
    dot_general x5, matrix products, onehot_sum(): jnp.dot(pattern, low_part, preferred_element_type=jnp.float32)  5.08 us
    dot_general x7, matrix products, first_dot(): lax.dot_general(left, right, (((0,), (0,)), ((), ())), preferred_element_...  4.6 us
  transfers between devices with their start and end apart: 5, of which 3 were waited for; matrix products, arithmetic and copies ran while one was open for 12% of the time, Pallas kernels for 0%

commit v1 on v0

v1 whole, which is shorter than its diff:
```python
import functools
import math

import jax
import jax.numpy as jnp
from jax import lax
from jax.experimental import pallas as pl
from jax.experimental.pallas import tpu as pltpu
from jax.sharding import PartitionSpec as P

EPSILON = 1e-05
BF16 = jnp.bfloat16
F32 = jnp.float32
MESH = pl.DeviceIdType.MESH
TILE = 16
BLOCK = 64


def last_dot(left, right):
    return lax.dot_general(left, right, (((1,), (1,)), ((), ())), preferred_element_type=F32)


def first_dot(left, right):
    return lax.dot_general(left, right, (((0,), (0,)), ((), ())), preferred_element_type=F32)


def onehot(index, count):
    rows = lax.broadcasted_iota(jnp.int32, (count, index.shape[1]), 0)
    return (rows == index).astype(F32).astype(BF16)


def norm_back(mixed, gain, upstream):
    centred = mixed - jnp.mean(mixed, -1, keepdims=True)
    inverse = lax.rsqrt(jnp.mean(centred * centred, -1, keepdims=True) + EPSILON)
    normed = centred * inverse
    scaled = upstream * gain
    delta = inverse * (
        scaled
        - jnp.mean(scaled, -1, keepdims=True)
        - normed * jnp.mean(scaled * normed, -1, keepdims=True)
    )
    return delta, normed


def stages_of(sizes):
    found = []
    for axis in ("dp", "space"):
        step = 1
        while step < sizes[axis]:
            found.append((axis, step))
            step *= 2
    return found


def halving_rows(rows, count):
    plan = []
    for _ in range(count):
        halves = (rows // 2) % TILE == 0
        rows = rows // 2 if halves else rows
        plan.append((rows, halves))
    return plan


def kernel(
    sizes,
    edge_scale,
    node_scale,
    node_latent,
    halo_latent,
    coarse_latent,
    edge_latent,
    edge_preact,
    edge_mixed,
    node_message,
    node_preact,
    node_mixed,
    edge_cotangent,
    node_cotangent,
    senders,
    receivers,
    send_rows,
    coarse_rows,
    edge_up,
    edge_down,
    edge_gain,
    node_up,
    node_down,
    node_gain,
    node_grad,
    edge_grad,
    edge_upgrad,
    edge_downgrad,
    node_upgrad,
    node_downgrad,
    edge_gaingrad,
    node_gaingrad,
    node_delta,
    node_hidden,
    node_signal,
    edge_delta,
    edge_hidden,
    edge_signal,
    edge_slope,
    sender_latent,
    receiver_latent,
    gathered,
    gain_sums,
    messages,
    edge_sent,
    edge_got,
    ext_own,
    ext_sent,
    ext_got,
    halo_sent,
    halo_got,
    coarse_sent,
    coarse_got,
    up_total,
    up_sent,
    up_got,
    down_total,
    down_sent,
    down_got,
    gain_sent,
    gain_got,
    sum_send,
    sum_recv,
    mp_send,
    mp_recv,
    halo_send,
    halo_recv,
    coarse_send,
    coarse_recv,
):
    mp, regions = sizes["mp"], sizes["space"]
    width = node_latent.shape[2]
    nodes = node_latent.shape[1]
    edges = edge_latent.shape[1]
    halo = halo_latent.shape[1] // 2
    coarse = coarse_latent.shape[1]
    owned = coarse // regions
    quarter = width // mp
    region = lax.axis_index("space")
    feature = lax.axis_index("mp")
    stages = stages_of(sizes)

    def beside(axis, shift):
        return lax.rem(lax.axis_index(axis) + shift, sizes[axis])

    barrier = pltpu.get_barrier_semaphore()
    for axis in ("mp", "dp", "space"):
        for shift in range(1, sizes[axis]):
            pl.semaphore_signal(
                barrier, inc=1, device_id={axis: beside(axis, shift)}, device_id_type=MESH
            )

    def remote(source, target, send, recv, axis, place):
        return pltpu.make_async_remote_copy(
            src_ref=source,
            dst_ref=target,
            send_sem=send,
            recv_sem=recv,
            device_id={axis: place},
            device_id_type=MESH,
        )

    def partner_of(axis, step):
        mine = lax.axis_index(axis)
        bit = lax.rem(mine // step, 2)
        return bit, mine + step - 2 * step * bit

    def summed(slot, total, sent, got, out, base, scale):
        rows = total.shape[0]
        start, held, filled = jnp.int32(0), rows, 0
        back = []
        for number, (axis, step) in enumerate(stages):
            count, halves = halving_rows(rows, len(stages))[number]
            bit, partner = partner_of(axis, step)
            place = pl.ds(filled, count)
            if halves:
                keep, give = start + bit * count, start + (1 - bit) * count
            else:
                keep = give = start
            keep, give = pl.multiple_of(keep, count), pl.multiple_of(give, count)
            sent[place, :] = total[pl.ds(give, count), :].astype(BF16)
            copy = remote(
                sent.at[place],
                got.at[place],
                sum_send.at[slot, number],
                sum_recv.at[slot, number],
                axis,
                partner,
            )
            copy.start()
            yield
            copy.wait()
            if halves:
                mine = total[pl.ds(keep, count), :]
                back.append((number, axis, partner, start))
            else:
                mine = sent[place, :].astype(F32)
            total[pl.ds(keep, count), :] = mine + got[place, :].astype(F32)
            start, held, filled = keep, count, filled + count
        final = pl.ds(pl.multiple_of(base + start, held), held)
        out[final, :] = (total[pl.ds(start, held), :] * scale).astype(BF16)
        for number, axis, partner, before in reversed(back):
            place = pl.ds(pl.multiple_of(base + start, held), held)
            copy = remote(
                out.at[place],
                out.at[place],
                sum_send.at[slot, len(stages) + number],
                sum_recv.at[slot, len(stages) + number],
                axis,
                partner,
            )
            copy.start()
            yield
            copy.wait()
            start, held = before, 2 * held

    def summed_gains(slot):
        value = gain_sums[...]
        for number, (axis, step) in enumerate(stages):
            _, partner = partner_of(axis, step)
            gain_sent[number] = value
            copy = remote(
                gain_sent.at[number],
                gain_got.at[number],
                sum_send.at[slot, number],
                sum_recv.at[slot, number],
                axis,
                partner,
            )
            copy.start()
            yield
            copy.wait()
            value = value + gain_got[number]
        edge_gaingrad[...] = value[0:1] * edge_scale
        node_gaingrad[...] = value[1:2] * node_scale

    running = []

    def begin(steps):
        next(steps)
        running.append(steps)

    def advance(times=1):
        for _ in range(times):
            for steps in list(running):
                if next(steps, "done") == "done":
                    running.remove(steps)

    def up_chunk(slot, value, out, base, scale):
        up_total[slot] = value
        begin(
            summed(slot, up_total.at[slot], up_sent.at[slot], up_got.at[slot], out, base, scale)
        )

    def down_chunk(slot, value, out, scale):
        down_total[slot] = value
        begin(
            summed(
                5 + slot, down_total.at[slot], down_sent.at[slot], down_got.at[slot], out, 0, scale
            )
        )

    gain_sums[...] = jnp.zeros_like(gain_sums)

    def node_rows(number, _):
        rows = pl.ds(pl.multiple_of(number * BLOCK, BLOCK), BLOCK)
        upstream = node_cotangent[0, rows, :].astype(F32)
        delta, normed = norm_back(node_mixed[0, rows, :].astype(F32), node_gain[...], upstream)
        gain_sums[1:2, :] += jnp.sum(upstream * normed, 0, keepdims=True)
        delta = delta.astype(BF16)
        node_delta[rows, :] = delta
        act = node_preact[0, rows, :].astype(F32)
        logistic = jax.nn.sigmoid(act)
        node_hidden[rows, :] = (act * logistic).astype(BF16)
        slope = logistic * (1.0 + act * (1.0 - logistic))
        node_signal[rows, :] = (last_dot(delta, node_down[...]) * slope).astype(BF16)
        return 0

    lax.fori_loop(0, nodes // BLOCK, node_rows, 0)
    messages[feature] = last_dot(node_signal[...], node_up[width:, :]).astype(BF16)

    pl.semaphore_wait(barrier, (mp - 1) + (sizes["dp"] - 1) + (regions - 1))
    message_copies = []
    for shift in range(1, mp):
        copy = remote(
            messages.at[feature],
            messages.at[feature],
            mp_send.at[0, shift],
            mp_recv.at[0, shift],
            "mp",
            beside("mp", shift),
        )
        copy.start()
        message_copies.append(copy)

    down_chunk(1, first_dot(node_hidden[...], node_delta[...]), node_downgrad, node_scale)
    up_chunk(3, first_dot(node_latent[0], node_signal[...]), node_upgrad, 0, node_scale)
    up_chunk(4, first_dot(node_message[0], node_signal[...]), node_upgrad, width, node_scale)

    receiver_hot = onehot(receivers[...], nodes)
    sender_hot = onehot(senders[...], nodes + 2 * halo + coarse)
    advance()

    def edge_acts(number, _):
        rows = pl.ds(pl.multiple_of(number * BLOCK, BLOCK), BLOCK)
        act = edge_preact[0, rows, :].astype(F32)
        logistic = jax.nn.sigmoid(act)
        edge_hidden[rows, :] = (act * logistic).astype(BF16)
        edge_slope[rows, :] = logistic * (1.0 + act * (1.0 - logistic))
        return 0

    lax.fori_loop(0, edges // BLOCK, edge_acts, 0)
    advance()
    receiver_latent[...] = first_dot(receiver_hot, node_latent[0]).astype(BF16)
    extended = jnp.concatenate([node_latent[0], halo_latent[0], coarse_latent[0]], 0)
    sender_latent[...] = first_dot(sender_hot, extended).astype(BF16)
    advance()

    for copy in message_copies:
        copy.wait()
    message = messages[0].astype(F32)
    for slot in range(1, mp):
        message = message + messages[slot].astype(F32)
    gathered[...] = first_dot(receiver_hot, message.astype(BF16))

    def edge_rows(number, _):
        rows = pl.ds(pl.multiple_of(number * BLOCK, BLOCK), BLOCK)
        upstream = edge_cotangent[0, rows, :].astype(F32) + gathered[rows, :]
        delta, normed = norm_back(edge_mixed[0, rows, :].astype(F32), edge_gain[...], upstream)
        gain_sums[0:1, :] += jnp.sum(upstream * normed, 0, keepdims=True)
        delta = delta.astype(BF16)
        edge_delta[rows, :] = delta
        edge_signal[rows, :] = (last_dot(delta, edge_down[...]) * edge_slope[rows, :]).astype(BF16)
        return 0

    lax.fori_loop(0, edges // BLOCK, edge_rows, 0)
    advance()
    down_chunk(0, first_dot(edge_hidden[...], edge_delta[...]), edge_downgrad, edge_scale)

    def weight_rows(block, place):
        return pl.ds(pl.multiple_of(block * width + place * quarter, quarter), quarter)

    def ext_part(place):
        signal = edge_signal[...]
        from_senders = last_dot(signal, edge_up[weight_rows(1, place), :]).astype(BF16)
        from_receivers = last_dot(signal, edge_up[weight_rows(2, place), :]).astype(BF16)
        ext = jnp.dot(sender_hot, from_senders, preferred_element_type=F32)
        node = jnp.dot(receiver_hot, from_receivers, preferred_element_type=F32)
        node = node + last_dot(node_signal[...], node_up[weight_rows(0, place), :])
        return ext[:nodes] + node, ext[nodes:]

    ext_copies, edge_copies = [], []
    for shift in range(1, mp):
        place = beside("mp", shift)
        node, ext = ext_part(place)
        ext_sent[shift, :nodes, :] = node.astype(BF16)
        ext_sent[shift, nodes:, :] = ext.astype(BF16)
        copy = remote(
            ext_sent.at[shift],
            ext_got.at[shift],
            mp_send.at[1, shift],
            mp_recv.at[1, shift],
            "mp",
            place,
        )
        copy.start()
        ext_copies.append(copy)
    up_chunk(0, first_dot(edge_latent[0], edge_signal[...]), edge_upgrad, 0, edge_scale)
    up_chunk(1, first_dot(sender_latent[...], edge_signal[...]), edge_upgrad, width, edge_scale)
    up_chunk(
        2, first_dot(receiver_latent[...], edge_signal[...]), edge_upgrad, 2 * width, edge_scale
    )
    begin(summed_gains(7))
    advance()
    for shift in range(1, mp):
        place = beside("mp", shift)
        part = last_dot(edge_signal[...], edge_up[weight_rows(0, place), :])
        edge_sent[shift] = part.astype(BF16)
        copy = remote(
            edge_sent.at[shift],
            edge_got.at[shift],
            mp_send.at[2, shift],
            mp_recv.at[2, shift],
            "mp",
            place,
        )
        copy.start()
        edge_copies.append(copy)
    node, ext = ext_part(feature)
    ext_own[:nodes, :] = node
    ext_own[nodes:, :] = ext
    advance()

    for copy in ext_copies:
        copy.wait()
    ext = ext_own[nodes:, :]
    for shift in range(1, mp):
        ext = ext + ext_got[shift, nodes:, :].astype(F32)
    halo_sent[...] = ext[: 2 * halo].astype(BF16)
    coarse_sent[...] = ext[2 * halo :]
    far_copies = []
    for slot, shift in enumerate((regions - 1, 1)):
        rows = pl.ds(slot * halo, halo)
        copy = remote(
            halo_sent.at[rows],
            halo_got.at[rows],
            halo_send.at[slot],
            halo_recv.at[slot],
            "space",
            beside("space", shift),
        )
        copy.start()
        far_copies.append(copy)
    for shift in range(1, regions):
        place = beside("space", shift)
        rows = pl.ds(pl.multiple_of(place * owned, owned), owned)
        copy = remote(
            coarse_sent.at[rows],
            coarse_got.at[shift],
            coarse_send.at[shift],
            coarse_recv.at[shift],
            "space",
            place,
        )
        copy.start()
        far_copies.append(copy)
    advance()

    columns = pl.ds(pl.multiple_of(feature * quarter, quarter), quarter)
    part = last_dot(edge_signal[...], edge_up[weight_rows(0, feature), :])
    part = part + edge_cotangent[0, :, columns].astype(F32)
    for copy in edge_copies:
        copy.wait()
    for shift in range(1, mp):
        part = part + edge_got[shift].astype(F32)
    edge_grad[0] = part.astype(BF16)
    advance()

    total = ext_own[:nodes, :] + node_cotangent[0, :, columns].astype(F32)
    for shift in range(1, mp):
        total = total + ext_got[shift, :nodes, :].astype(F32)
    for copy in far_copies:
        copy.wait()
    total = total + jnp.dot(
        onehot(send_rows[...], nodes), halo_got[...], preferred_element_type=F32
    )
    own_coarse = coarse_sent[pl.ds(pl.multiple_of(region * owned, owned), owned), :]
    for shift in range(1, regions):
        own_coarse = own_coarse + coarse_got[shift]
    own_coarse = jnp.concatenate([own_coarse.astype(BF16).astype(F32)] * regions, 0).astype(BF16)
    owner = lax.broadcasted_iota(jnp.int32, (1, coarse), 1) // owned
    coarse_hot = onehot(jnp.where(owner == region, coarse_rows[...], -1), nodes)
    total = total + jnp.dot(coarse_hot, own_coarse, preferred_element_type=F32)
    node_grad[0] = total.astype(BF16)
    while running:
        advance()


def body(sizes, *arguments):
    (node_latent, halo_latent, coarse_latent, edge_latent, edge_preact) = arguments[:5]
    senders, receivers, send_rows, coarse_rows = arguments[11:15]
    edge_up, edge_down, edge_gain, node_up, node_down, node_gain = arguments[15:]
    width = node_latent.shape[2]
    nodes = node_latent.shape[1]
    edges = edge_latent.shape[1]
    halo_rows = halo_latent.shape[1]
    coarse = coarse_latent.shape[1]
    hidden = edge_preact.shape[2]
    mp, regions = sizes["mp"], sizes["space"]
    quarter = width // mp
    owned = coarse // regions
    extended = nodes + halo_rows + coarse
    stages = len(stages_of(sizes))
    samples = node_latent.shape[0] * sizes["dp"]
    edge_scale = 1.0 / math.sqrt(samples * edges * regions)
    node_scale = 1.0 / math.sqrt(samples * nodes * regions)
    up_rows = sum(rows for rows, _ in halving_rows(width, stages))
    down_rows = sum(rows for rows, _ in halving_rows(hidden, stages))
    shape = jax.ShapeDtypeStruct
    vmem = pltpu.VMEM
    semaphores = pltpu.SemaphoreType.DMA
    out_shape = (
        shape((1, nodes, quarter), BF16),
        shape((1, edges, quarter), BF16),
        shape((3 * width, hidden), BF16),
        shape((hidden, width), BF16),
        shape((2 * width, hidden), BF16),
        shape((hidden, width), BF16),
        shape((1, width), F32),
        shape((1, width), F32),
    )
    scratch = [
        vmem((nodes, width), BF16),
        vmem((nodes, hidden), BF16),
        vmem((nodes, hidden), BF16),
        vmem((edges, width), BF16),
        vmem((edges, hidden), BF16),
        vmem((edges, hidden), BF16),
        vmem((edges, hidden), F32),
        vmem((edges, width), BF16),
        vmem((edges, width), BF16),
        vmem((edges, width), F32),
        vmem((8, width), F32),
        vmem((mp, nodes, width), BF16),
        vmem((mp, edges, quarter), BF16),
        vmem((mp, edges, quarter), BF16),
        vmem((extended, quarter), F32),
        vmem((mp, extended, quarter), BF16),
        vmem((mp, extended, quarter), BF16),
        vmem((halo_rows, quarter), BF16),
        vmem((halo_rows, quarter), BF16),
        vmem((coarse, quarter), F32),
        vmem((regions, owned, quarter), F32),
        vmem((5, width, hidden), F32),
        vmem((5, up_rows, hidden), BF16),
        vmem((5, up_rows, hidden), BF16),
        vmem((2, hidden, width), F32),
        vmem((2, down_rows, width), BF16),
        vmem((2, down_rows, width), BF16),
        vmem((stages, 8, width), F32),
        vmem((stages, 8, width), F32),
        semaphores((8, 2 * stages)),
        semaphores((8, 2 * stages)),
        semaphores((3, mp)),
        semaphores((3, mp)),
        semaphores((2,)),
        semaphores((2,)),
        semaphores((regions,)),
        semaphores((regions,)),
    ]
    operands = arguments[:11] + (
        senders.reshape(1, -1),
        receivers.reshape(1, -1),
        send_rows.reshape(1, -1),
        coarse_rows.reshape(1, -1),
        edge_up,
        edge_down,
        edge_gain.reshape(1, -1),
        node_up,
        node_down,
        node_gain.reshape(1, -1),
    )
    outs = pl.pallas_call(
        functools.partial(kernel, sizes, edge_scale, node_scale),
        out_shape=out_shape,
        in_specs=[pl.BlockSpec(memory_space=vmem)] * len(operands),
        out_specs=tuple([pl.BlockSpec(memory_space=vmem)] * len(out_shape)),
        scratch_shapes=scratch,
        compiler_params=pltpu.CompilerParams(
            collective_id=0, has_side_effects=True, vmem_limit_bytes=56 * 1024 * 1024
        ),
    )(*operands)
    return outs[:6] + (outs[6].reshape(-1), outs[7].reshape(-1))


def solution(mesh):
    sizes = {axis: mesh.shape[axis] for axis in ("space", "dp", "mp")}
    return jax.shard_map(
        functools.partial(body, sizes),
        mesh=mesh,
        in_specs=(
            P(("group", "dp"), "space", None),
            P(("group", "dp"), "space", None),
            P(("group", "dp"), None, None),
            P(("group", "dp"), "space", None),
            P(("group", "dp"), "space", "mp"),
            P(("group", "dp"), "space", None),
            P(("group", "dp"), "space", None),
            P(("group", "dp"), "space", "mp"),
            P(("group", "dp"), "space", None),
            P(("group", "dp"), "space", None),
            P(("group", "dp"), "space", None),
            P("space"),
            P("space"),
            P("space", None, None),
            P(),
            P(None, "mp"),
            P("mp", None),
            P(),
            P(None, "mp"),
            P("mp", None),
            P(),
        ),
        out_specs=(
            P(("group", "dp"), "space", "mp"),
            P(("group", "dp"), "space", "mp"),
            P("group", "mp"),
            P(("group", "mp"), None),
            P("group", "mp"),
            P(("group", "mp"), None),
            P("group"),
            P("group"),
        ),
        check_vma=False,
    )
```

time: 228 us -> 65.9 us (0.29)
  waiting for transfers between devices: 120 us -> 0 us
  Pallas kernels: 0 us -> 56.3 us
  blocking collectives: 37 us -> 0 us
  other arithmetic: 17.4 us -> 0 us
  matrix products: 16.7 us -> 0 us
  between operations: 14.2 us -> 0.67 us
  local copies, waits for them, and re-layouts: 18.4 us -> 8.6 us
  starting transfers between devices: 3.45 us -> 0 us
    psum x2 -> x0, waiting for transfers between devices: 98.3 us -> none  [the longest x1 64.6 us: body(): lax.psum((edge_upsum, edge_downsum, node_upsum, node_downsum, edge_gainsu...]
    pallas_call x0 -> x1, Pallas kernels: none -> 56.3 us  [body(): pl.pallas_call(functools.partial(kernel, sizes, edge_scale, node_scale),...]
    psum x2 -> x0, blocking collectives: 37 us -> none  [the longest x1 19.8 us: body(): lax.psum(coarse_grad.astype(jnp.bfloat16), 'space').astype(jnp.float32)]
    reduce_scatter x1 -> x0, waiting for transfers between devices: 22.1 us -> none  [body(): lax.psum_scatter(edge_terms.astype(jnp.bfloat16), 'mp', scatter_dimension...]
    dot_general x21 -> x0, matrix products: 16.7 us -> none  [the longest x5 5.08 us: onehot_sum(): jnp.dot(pattern, low_part, preferred_element_type=jnp.float32)]
    convert_element_type x6 -> x0, other arithmetic: 7.27 us -> none  [the longest x1 1.78 us: body(): (totals[1] * edge_scale).astype(jnp.bfloat16)]
    gather x3 -> x0, local copies, waits for them, and re-layouts: 6.87 us -> none  [the longest x1 2.63 us: body(): sender_latent = jnp.take(extended, senders, axis=0)]
    reduce_sum x6 -> x0, other arithmetic: 5.9 us -> none  [the longest x1 1.77 us: body(): edge_gainsum = jnp.sum(edge_upstream * edge_normed, 0)]
  transfers between devices with their start and end apart: 5 -> 0, of which waited for: 3 -> 0; matrix products, arithmetic and copies ran while one was open for 12% -> 0% of each run, Pallas kernels for 0% -> 0%
where the time goes in v1:
time: 65.9 us; the launch traced here: 65.5 us
  Pallas kernels  56.3 us (85%)
  local copies, waits for them, and re-layouts  8.6 us (13%)
  between operations  0.67 us (1%)
    pallas_call x1, Pallas kernels, body(): pl.pallas_call(functools.partial(kernel, sizes, edge_scale, node_scale),...  56.3 us
    unnamed x20, local copies, waits for them, and re-layouts  8.6 us

profile of v1, /device:TPU:0, one launch (start us, length us, event | category | flops | bytes accessed | tf_op | source)
XLA Modules:
  0.0 65.5 jit_solution(16251916190727714531)
XLA Ops:
  0.6 56.3 %shard_map.260 = (bf16[1,256,256]{2,1,0:T(8,128)(2,1)}, bf16[1,512,256]{2,1,0:T(8,128)(2,1)}, bf16[1536,256]{1,0:T(8,128)(2,1)}, bf16[256,512]{1,0:T(8,128)(2,1)...) custom-call(bf16[1,256,512]{2,1,0:T(8,128)(2,1)} %node_latent.1, ...), custom_call_target="tpu_custom_call" | custom-call | tf_op jit(solution)/shard_map/pallas_call | solution.py:547
  56.9 0.0 copy-start
  56.9 1.6 %copy.37 = bf16[1,256,256]{2,1,0:T(8,128)(2,1)} copy(bf16[1,256,256]{2,1,0:T(8,128)(2,1)} %get-tuple-element.32) | data formatting | bytes 262144
  58.6 1.7 %copy.38 = bf16[1,512,256]{2,1,0:T(8,128)(2,1)} copy(bf16[1,512,256]{2,1,0:T(8,128)(2,1)} %get-tuple-element.33) | data formatting | bytes 524288
  60.2 0.0 copy-done
  60.2 0.0 copy-start.3
  60.2 0.9 %copy.39 = bf16[1536,256]{1,0:T(8,128)(2,1)} copy(bf16[1536,256]{1,0:T(8,128)(2,1)S(1)} %copy-done) | data formatting | bytes 1572864
  61.1 0.2 copy-done.3
  61.3 0.0 copy-start.1
  61.3 0.7 %copy.40 = bf16[256,512]{1,0:T(8,128)(2,1)} copy(bf16[256,512]{1,0:T(8,128)(2,1)S(1)} %copy-done.3) | data formatting | bytes 524288
  62.0 0.4 copy-done.1
  62.5 0.0 copy-start.2
  62.5 0.8 %copy.41 = bf16[1024,256]{1,0:T(8,128)(2,1)} copy(bf16[1024,256]{1,0:T(8,128)(2,1)S(1)} %copy-done.1) | data formatting | bytes 1048576
  63.3 0.3 copy-done.2
  63.6 0.0 copy-start.5
  63.6 0.7 %copy.42 = bf16[256,512]{1,0:T(8,128)(2,1)} copy(bf16[256,512]{1,0:T(8,128)(2,1)S(1)} %copy-done.2) | data formatting | bytes 524288
  64.3 0.0 copy-done.5
  64.3 0.0 copy-start.4
  64.3 0.6 copy.43
  64.9 0.1 copy-done.4
  65.0 0.6 copy.44
Async XLA Ops:
  56.9 3.3 %copy-start = (bf16[1536,256]{1,0:T(8,128)(2,1)S(1)}, bf16[1536,256]{1,0:T(8,128)(2,1)}, u32[]{:S(2)}) copy-start(bf16[1536,256]{1,0:T(8,128)(2,1)} %get-tuple-element.34) | copy-start | bytes 2359300
  60.2 1.1 %copy-start.3 = (bf16[256,512]{1,0:T(8,128)(2,1)S(1)}, bf16[256,512]{1,0:T(8,128)(2,1)}, u32[]{:S(2)}) copy-start(bf16[256,512]{1,0:T(8,128)(2,1)} %get-tuple-element.35) | copy-start | bytes 786436
  61.3 1.1 %copy-start.1 = (bf16[1024,256]{1,0:T(8,128)(2,1)S(1)}, bf16[1024,256]{1,0:T(8,128)(2,1)}, u32[]{:S(2)}) copy-start(bf16[1024,256]{1,0:T(8,128)(2,1)} %get-tuple-element.36) | copy-start | bytes 1572868
  62.5 1.1 %copy-start.2 = (bf16[256,512]{1,0:T(8,128)(2,1)S(1)}, bf16[256,512]{1,0:T(8,128)(2,1)}, u32[]{:S(2)}) copy-start(bf16[256,512]{1,0:T(8,128)(2,1)} %get-tuple-element.37) | copy-start | bytes 786436
  63.6 0.7 %copy-start.5 = (f32[1,512]{1,0:T(1,128)S(1)}, f32[1,512]{1,0:T(1,128)}, u32[]{:S(2)}) copy-start(f32[1,512]{1,0:T(1,128)} %get-tuple-element.22) | copy-start | bytes 6148
  64.3 0.7 %copy-start.4 = (f32[1,512]{1,0:T(1,128)S(1)}, f32[1,512]{1,0:T(1,128)}, u32[]{:S(2)}) copy-start(f32[1,512]{1,0:T(1,128)} %get-tuple-element.23) | copy-start | bytes 6148

commit v2 on v1

--- a/solution.py
+++ b/solution.py
@@ -61,10 +61,41 @@
     return plan
 
 
+ORDER = (
+    "node_mixed",
+    "node_cotangent",
+    "node_gain",
+    "node_preact",
+    "node_down",
+    "node_up",
+    "node_latent",
+    "node_message",
+    "receivers",
+    "senders",
+    "edge_preact",
+    "halo_latent",
+    "coarse_latent",
+    "edge_cotangent",
+    "edge_mixed",
+    "edge_gain",
+    "edge_down",
+    "edge_up",
+    "edge_latent",
+    "send_rows",
+    "coarse_rows",
+)
+
+
+def staged_kernel(sizes, edge_scale, node_scale, inputs, *refs):
+    places = refs[-inputs:]
+    kernel(sizes, edge_scale, node_scale, refs[:inputs], *places, *refs[inputs:-inputs])
+
+
 def kernel(
     sizes,
     edge_scale,
     node_scale,
+    operands,
     node_latent,
     halo_latent,
     coarse_latent,
@@ -131,8 +162,43 @@
     halo_recv,
     coarse_send,
     coarse_recv,
+    load_sem,
 ):
     mp, regions = sizes["mp"], sizes["space"]
+    held = {
+        "node_latent": node_latent,
+        "halo_latent": halo_latent,
+        "coarse_latent": coarse_latent,
+        "edge_latent": edge_latent,
+        "edge_preact": edge_preact,
+        "edge_mixed": edge_mixed,
+        "node_message": node_message,
+        "node_preact": node_preact,
+        "node_mixed": node_mixed,
+        "edge_cotangent": edge_cotangent,
+        "node_cotangent": node_cotangent,
+        "senders": senders,
+        "receivers": receivers,
+        "send_rows": send_rows,
+        "coarse_rows": coarse_rows,
+        "edge_up": edge_up,
+        "edge_down": edge_down,
+        "edge_gain": edge_gain,
+        "node_up": node_up,
+        "node_down": node_down,
+        "node_gain": node_gain,
+    }
+    loads = {
+        name: pltpu.make_async_copy(operands[place], held[name], load_sem.at[place])
+        for place, name in enumerate(held)
+    }
+    for name in ORDER:
+        loads[name].start()
+
+    def ready(*names):
+        for name in names:
+            loads.pop(name).wait()
+
     width = node_latent.shape[2]
     nodes = node_latent.shape[1]
     edges = edge_latent.shape[1]
@@ -266,6 +332,8 @@
 
     gain_sums[...] = jnp.zeros_like(gain_sums)
 
+    ready("node_mixed", "node_cotangent", "node_gain", "node_preact", "node_down")
+
     def node_rows(number, _):
         rows = pl.ds(pl.multiple_of(number * BLOCK, BLOCK), BLOCK)
         upstream = node_cotangent[0, rows, :].astype(F32)
@@ -281,6 +349,7 @@
         return 0
 
     lax.fori_loop(0, nodes // BLOCK, node_rows, 0)
+    ready("node_up")
     messages[feature] = last_dot(node_signal[...], node_up[width:, :]).astype(BF16)
 
     pl.semaphore_wait(barrier, (mp - 1) + (sizes["dp"] - 1) + (regions - 1))
@@ -297,13 +366,14 @@
         copy.start()
         message_copies.append(copy)
 
+    ready("node_latent", "node_message")
     down_chunk(1, first_dot(node_hidden[...], node_delta[...]), node_downgrad, node_scale)
     up_chunk(3, first_dot(node_latent[0], node_signal[...]), node_upgrad, 0, node_scale)
     up_chunk(4, first_dot(node_message[0], node_signal[...]), node_upgrad, width, node_scale)
 
+    ready("senders", "receivers", "edge_preact", "halo_latent", "coarse_latent")
     receiver_hot = onehot(receivers[...], nodes)
     sender_hot = onehot(senders[...], nodes + 2 * halo + coarse)
-    advance()
 
     def edge_acts(number, _):
         rows = pl.ds(pl.multiple_of(number * BLOCK, BLOCK), BLOCK)
@@ -318,14 +388,15 @@
     receiver_latent[...] = first_dot(receiver_hot, node_latent[0]).astype(BF16)
     extended = jnp.concatenate([node_latent[0], halo_latent[0], coarse_latent[0]], 0)
     sender_latent[...] = first_dot(sender_hot, extended).astype(BF16)
-    advance()
-
+
+    ready(*tuple(loads))
     for copy in message_copies:
         copy.wait()
     message = messages[0].astype(F32)
     for slot in range(1, mp):
         message = message + messages[slot].astype(F32)
     gathered[...] = first_dot(receiver_hot, message.astype(BF16))
+    advance()
 
     def edge_rows(number, _):
         rows = pl.ds(pl.multiple_of(number * BLOCK, BLOCK), BLOCK)
@@ -338,7 +409,6 @@
         return 0
 
     lax.fori_loop(0, edges // BLOCK, edge_rows, 0)
-    advance()
     down_chunk(0, first_dot(edge_hidden[...], edge_delta[...]), edge_downgrad, edge_scale)
 
     def weight_rows(block, place):
@@ -375,7 +445,6 @@
         2, first_dot(receiver_latent[...], edge_signal[...]), edge_upgrad, 2 * width, edge_scale
     )
     begin(summed_gains(7))
-    advance()
     for shift in range(1, mp):
         place = beside("mp", shift)
         part = last_dot(edge_signal[...], edge_up[weight_rows(0, place), :])
@@ -393,7 +462,7 @@
     node, ext = ext_part(feature)
     ext_own[:nodes, :] = node
     ext_own[nodes:, :] = ext
-    advance()
+    advance(2)
 
     for copy in ext_copies:
         copy.wait()
@@ -458,6 +527,30 @@
     node_grad[0] = total.astype(BF16)
     while running:
         advance()
+
+
+def copy_kernel(*refs):
+    count = len(refs) // 2
+    sems = refs[-1]
+    copies = [
+        pltpu.make_async_copy(refs[place], refs[count + place], sems.at[place])
+        for place in range(count)
+    ]
+    for copy in copies:
+        copy.start()
+    for copy in copies:
+        copy.wait()
+
+
+def copied(arrays):
+    count = len(arrays)
+    return pl.pallas_call(
+        copy_kernel,
+        out_shape=tuple(jax.ShapeDtypeStruct(array.shape, array.dtype) for array in arrays),
+        in_specs=[pl.BlockSpec(memory_space=pltpu.VMEM)] * count,
+        out_specs=tuple([pl.BlockSpec(memory_space=pl.ANY)] * count),
+        scratch_shapes=[pltpu.SemaphoreType.DMA((count,))],
+    )(*arrays)
 
 
 def body(sizes, *arguments):
@@ -531,6 +624,7 @@
         semaphores((2,)),
         semaphores((regions,)),
         semaphores((regions,)),
+        semaphores((len(ORDER),)),
     ]
     operands = arguments[:11] + (
         senders.reshape(1, -1),
@@ -545,16 +639,17 @@
         node_gain.reshape(1, -1),
     )
     outs = pl.pallas_call(
-        functools.partial(kernel, sizes, edge_scale, node_scale),
+        functools.partial(staged_kernel, sizes, edge_scale, node_scale, len(operands)),
         out_shape=out_shape,
-        in_specs=[pl.BlockSpec(memory_space=vmem)] * len(operands),
+        in_specs=[pl.BlockSpec(memory_space=pl.ANY)] * len(operands),
         out_specs=tuple([pl.BlockSpec(memory_space=vmem)] * len(out_shape)),
-        scratch_shapes=scratch,
+        scratch_shapes=scratch + [vmem(array.shape, array.dtype) for array in operands],
         compiler_params=pltpu.CompilerParams(
             collective_id=0, has_side_effects=True, vmem_limit_bytes=56 * 1024 * 1024
         ),
     )(*operands)
-    return outs[:6] + (outs[6].reshape(-1), outs[7].reshape(-1))
+    outs = copied(outs)
+    return tuple(outs[:6]) + (outs[6].reshape(-1), outs[7].reshape(-1))
 
 
 def solution(mesh):

time: 65.9 us -> 57.5 us (0.87)
  local copies, waits for them, and re-layouts: 8.6 us -> 0 us
    unnamed x20 -> x0, local copies, waits for them, and re-layouts: 8.6 us -> none
    pallas_call x1 -> x2, Pallas kernels: 56.3 us -> 56.7 us  [the longest x1 53.8 us: body(): pl.pallas_call(functools.partial(staged_kernel, sizes, edge_scale, node_s...]
where the time goes in v2:
time: 57.5 us; the launch traced here: 57.4 us
  Pallas kernels  56.7 us (99%)
  between operations  0.65 us (1%)
    pallas_call x1, Pallas kernels, body(): pl.pallas_call(functools.partial(staged_kernel, sizes, edge_scale, node_s...  53.8 us
    pallas_call x1, Pallas kernels, copied(): pl.pallas_call(copy_kernel, out_shape=tuple((jax.ShapeDtypeStruct(array.s...  2.99 us

profile of v2, /device:TPU:0, one launch (start us, length us, event | category | flops | bytes accessed | tf_op | source)
XLA Modules:
  0.0 57.4 jit_solution(9594049992875321213)
XLA Ops:
  0.6 53.8 %shard_map.260 = (bf16[1,256,256]{2,1,0:T(8,128)(2,1)}, bf16[1,512,256]{2,1,0:T(8,128)(2,1)}, bf16[1536,256]{1,0:T(8,128)(2,1)}, bf16[256,512]{1,0:T(8,128)(2,1)...) custom-call(bf16[1,256,512]{2,1,0:T(8,128)(2,1)} %refs_0_.1, ...), custom_call_target="tpu_custom_call" | custom-call | tf_op jit(solution)/shard_map/pallas_call | solution.py:641
  54.4 3.0 %shard_map.261 = (bf16[1,256,256]{2,1,0:T(8,128)(2,1)}, bf16[1,512,256]{2,1,0:T(8,128)(2,1)}, bf16[1536,256]{1,0:T(8,128)(2,1)}, bf16[256,512]{1,0:T(8,128)(2,1)...) custom-call(bf16[1,256,256]{2,1,0:T(8,128)(2,1)} %get-tuple-element.24.refs_0_, ...), custom_call_target="tpu_custom_call" | custom-call | tf_op jit(solution)/shard_map/pallas_call | solution.py:547
